TPU v7x, 32 devices: a whole 2x2x4 slice. The times are simulated.
32 devices in a mesh: blk: 8 (over y, x, core), req: 4 (over z).
Axes of the slice: x: 2, y: 2, z: 4, core: 2. Of those that a mesh axis runs over, the one named last changes fastest.
Arguments:
- long_q: bfloat16 [8192, 2048], P('blk', 'req'), may hold values from -6 to 6
- long_k: bfloat16 [8192, 2048], P('blk', 'req'), may hold values from -6 to 6
- long_v: bfloat16 [8192, 2048], P('blk', 'req'), may hold values from -6 to 6
- short_q: bfloat16 [4096, 2048], P('blk', 'req'), may hold values from -6 to 6
- short_k: bfloat16 [4096, 2048], P('blk', 'req'), may hold values from -6 to 6
- short_v: bfloat16 [4096, 2048], P('blk', 'req'), may hold values from -6 to 6
- short_seg: int32 [8, 512], P('blk'), may hold values from 0 to 15, never falling along the last dimension, each value on 1 to 96 neighbouring positions
- pool_kv: bfloat16 [512, 2, 16, 2048], P('blk', None, None, 'req'), may hold values from -6 to 6
- page_table: int32 [8, 16, 4], replicated, may hold values from 0 to 511, as said below
- w_out: bfloat16 [2048, 2048], replicated, may hold values from -0.125 to 0.125
Outputs:
- long_out: bfloat16 [8192, 2048], P(('blk', 'req'))
- short_out: bfloat16 [4096, 2048], P(('blk', 'req'))
Inputs may be any that keep to these rules, and one draw needn't show every extreme that they name: `short_seg`: along each pack the request numbers never fall, and each of the 16 requests has 1 to 96 tokens, one of them exactly 96. `page_table`: entry [b, s, j] is o * 64 + i for page i of the pool rows held by index o of blk; for every pack b and every o exactly 8 of the 64 entries of b name pages of o.
All inputs are finite; a program needn't handle non-finite values.
Results may differ from a plain program's by a relative error of at most 0.015.
Values may be sent and summed in bfloat16 or wider, within the bound.
A program may use at most 128 MiB of HBM per device.

v0:
```python
import math

import jax
import jax.numpy as jnp
from jax import lax
from jax.sharding import PartitionSpec as P

HD = 128
PPS = 4


very_negative = -1e30


def fold_block(state_now, query_heads, query_pos, key_block, value_block, block_first):
    acc_sum, run_max, run_total = state_now
    heads_dev = query_heads.shape[1]
    key_heads = key_block.reshape(key_block.shape[0], heads_dev, HD)
    value_heads = value_block.reshape(value_block.shape[0], heads_dev, HD)
    scores = jnp.einsum(
        "qhd,khd->hqk", query_heads, key_heads, preferred_element_type=jnp.float32
    ) * HD ** (-0.5)
    key_pos = block_first + jnp.arange(key_block.shape[0], dtype=jnp.int32)
    allowed = (key_pos[None, :] <= query_pos[:, None])[None]
    scores = jnp.where(allowed, scores, very_negative)
    new_max = jnp.maximum(run_max, jnp.max(scores, axis=-1))
    weights = jnp.where(allowed, jnp.exp(scores - new_max[..., None]), 0.0)
    factor = jnp.exp(run_max - new_max)
    run_total = run_total * factor + jnp.sum(weights, axis=-1)
    acc_sum = acc_sum * factor[..., None] + jnp.einsum(
        "hqk,khd->hqd",
        weights.astype(jnp.bfloat16),
        value_heads,
        preferred_element_type=jnp.float32,
    )
    return (acc_sum, new_max, run_total)


def prompt_attention(queries, query_pos, long_k, long_v):
    row_count, width = queries.shape
    heads_dev = width // HD
    query_heads = queries.reshape(row_count, heads_dev, HD)
    last_pos = jnp.max(query_pos)
    init = (
        jnp.zeros((heads_dev, row_count, HD), jnp.float32),
        jnp.full((heads_dev, row_count), very_negative, jnp.float32),
        jnp.zeros((heads_dev, row_count), jnp.float32),
    )
    key_piece = lax.all_gather(long_k, "blk", axis=0, tiled=True)
    value_piece = lax.all_gather(long_v, "blk", axis=0, tiled=True)
    piece_rows = key_piece.shape[0]
    step_rows = math.gcd(piece_rows, 1024)

    def one_step(block_num, state_in):
        block_start = block_num * step_rows
        key_block = lax.dynamic_slice_in_dim(key_piece, block_start, step_rows, 0)
        value_block = lax.dynamic_slice_in_dim(value_piece, block_start, step_rows, 0)

        def compute_block(state_live):
            return fold_block(
                state_live, query_heads, query_pos, key_block, value_block, block_start
            )

        def keep_state(state_skip):
            return state_skip

        return lax.cond(block_start <= last_pos, compute_block, keep_state, state_in)

    acc_sum, run_max, run_total = lax.fori_loop(0, piece_rows // step_rows, one_step, init)
    merged = acc_sum / run_total[..., None]
    return merged.transpose(1, 0, 2).reshape(row_count, width).astype(jnp.bfloat16)


def pack_attention(
    short_q, short_k, short_v, short_seg, pool_kv, page_table, block_index, block_count
):
    pack_rows, width = short_q.shape
    heads_dev = width // HD
    pool_pages = pool_kv.shape[0]
    page_len = pool_kv.shape[2]
    page_rows = page_table.reshape(block_count, -1)
    entries = page_rows.shape[1]
    capacity = entries // block_count
    owners = page_rows // pool_pages
    places = page_rows % pool_pages
    wanted = owners == block_index
    ranks = jnp.cumsum(wanted.astype(jnp.int32), axis=1) - 1
    picked = wanted[:, :, None] & (
        ranks[:, :, None] == jnp.arange(capacity, dtype=jnp.int32)[None, None, :]
    )
    send_places = jnp.sum(jnp.where(picked, places[:, :, None], 0), axis=1)
    outgoing = pool_kv[send_places.reshape(-1)].reshape(block_count, capacity, 2, page_len, width)
    arrived = lax.all_to_all(outgoing, "blk", split_axis=0, concat_axis=0, tiled=True)
    my_owners = lax.dynamic_index_in_dim(owners, block_index, 0, keepdims=False)
    order = jnp.arange(entries, dtype=jnp.int32)
    before = (my_owners[None, :] == my_owners[:, None]) & (order[None, :] < order[:, None])
    slots = my_owners * capacity + jnp.sum(before.astype(jnp.int32), axis=1)
    fetched = arrived.reshape(block_count * capacity, 2, page_len, width)[slots]
    cache_len = entries * page_len
    key_rows = jnp.concatenate([fetched[:, 0].reshape(cache_len, width), short_k], 0)
    value_rows = jnp.concatenate([fetched[:, 1].reshape(cache_len, width), short_v], 0)
    segment = short_seg[0]
    positions = jnp.arange(pack_rows, dtype=jnp.int32)
    key_seg = jnp.concatenate([jnp.arange(cache_len, dtype=jnp.int32) // (PPS * page_len), segment])
    key_pos = jnp.concatenate([jnp.full((cache_len,), -1, jnp.int32), positions])
    allowed = ((key_seg[None, :] == segment[:, None]) & (key_pos[None, :] <= positions[:, None]))[
        None
    ]
    query_heads = short_q.reshape(pack_rows, heads_dev, HD)
    key_heads = key_rows.reshape(cache_len + pack_rows, heads_dev, HD)
    value_heads = value_rows.reshape(cache_len + pack_rows, heads_dev, HD)
    scores = jnp.einsum(
        "qhd,khd->hqk", query_heads, key_heads, preferred_element_type=jnp.float32
    ) * HD ** (-0.5)
    scores = jnp.where(allowed, scores, very_negative)
    row_max = jnp.max(scores, axis=-1)
    weights = jnp.where(allowed, jnp.exp(scores - row_max[..., None]), 0.0)
    total = jnp.sum(weights, axis=-1)
    numer = jnp.einsum(
        "hqk,khd->hqd",
        weights.astype(jnp.bfloat16),
        value_heads,
        preferred_element_type=jnp.float32,
    )
    merged = numer / total[..., None]
    return merged.transpose(1, 0, 2).reshape(pack_rows, width).astype(jnp.bfloat16)


def per_device(
    long_q, long_k, long_v, short_q, short_k, short_v, short_seg, pool_kv, page_table, w_out
):
    block_count = lax.axis_size("blk")
    block_index = lax.axis_index("blk")
    group_index = lax.axis_index("req")
    row_count, width = long_q.shape
    query_pos = block_index * row_count + jnp.arange(row_count, dtype=jnp.int32)
    long_attn = prompt_attention(long_q, query_pos, long_k, long_v)
    short_attn = pack_attention(
        short_q, short_k, short_v, short_seg, pool_kv, page_table, block_index, block_count
    )
    w_rows = lax.dynamic_slice_in_dim(w_out, group_index * width, width, 0)
    long_out = lax.psum_scatter(
        jnp.dot(long_attn, w_rows, preferred_element_type=jnp.float32).astype(jnp.bfloat16),
        "req",
        scatter_dimension=0,
        tiled=True,
    )
    short_out = lax.psum_scatter(
        jnp.dot(short_attn, w_rows, preferred_element_type=jnp.float32).astype(jnp.bfloat16),
        "req",
        scatter_dimension=0,
        tiled=True,
    )
    return (long_out, short_out)


def solution(mesh):
    placed = (
        P("blk", "req"),
        P("blk", "req"),
        P("blk", "req"),
        P("blk", "req"),
        P("blk", "req"),
        P("blk", "req"),
        P("blk", None),
        P("blk", None, None, "req"),
        P(),
        P(),
    )
    return jax.shard_map(
        per_device,
        mesh=mesh,
        in_specs=placed,
        out_specs=(P(("blk", "req"), None), P(("blk", "req"), None)),
        check_vma=False,
    )
```

profile of v0, /device:TPU:14, one launch (start us, length us, event | category | flops | bytes accessed | tf_op | source)
XLA Modules:
  0.0 403.1 jit_solution(5166171699062916849)
XLA Ops:
  8.1 2.4 copy.40
  10.6 2.3 copy.42
  13.7 2.0 gather_fusion
  15.7 4.2 %all-to-all-start = ((bf16[8,8,2,16,512]{4,3,2,1,0:T(8,128)(2,1)}), bf16[8,8,2,16,512]{4,3,2,1,0:T(8,128)(2,1)S(1)}, u32[]{:S(2)}, u32[]{:S(2)}) async-start(bf16[8,8,2,16,512]{4,3,2,1,0:T(8,128)(2,1)} %bitcast.74), calls=%async_computation.1 | async-start | bytes 4194304 | tf_op jit(solution)/shard_map/all_to_all | solution.py:93
  20.1 1.0 copy.52
  21.1 2.1 copy.54
  23.4 2.0 fusion.20
  25.4 30.0 %all-to-all-done = bf16[8,8,2,16,512]{4,3,2,1,0:T(8,128)(2,1)S(1)} async-done(((bf16[8,8,2,16,512]{4,3,2,1,0:T(8,128)(2,1)}), bf16[8,8,2,16,512]{4,3,2,1,0:T(8,128)(2,1)S(1)}, u32[]{:S(2)}, u32[]{:S(2)}) %all-to-all-start) | async-done | bytes 2097184 | tf_op jit(solution)/shard_map/all_to_all | solution.py:93
  55.4 2.0 gather_fusion.1
  57.4 1.7 fusion.58
  59.9 1.5 copy.55
  61.3 3.1 fusion.26
  64.4 9.6 %fusion.59 = (f32[4,512]{1,0:T(4,128)S(1)}, bf16[4,512,1536]{1,2,0:T(8,128)(2,1)}) fusion(f32[4,1536,512]{2,1,0:T(8,128)S(1)} %fusion.26, pred[512,1536]{0,1:T(8,128)(4,1)} %fusion.20), kind=kOutput, calls=%fused_computation.90 | output fusion | flops 25167360 | bytes 19668992 | tf_op jit(solution)/shard_map/sub | solution.py:117
  74.0 3.9 divide_convert_fusion.1
  78.0 4.3 %convolution_convert_fusion.1 = bf16[512,2048]{1,0:T(8,128)(2,1)} fusion(bf16[512,512]{0,1:T(8,128)(2,1)S(1)} %bitcast.78, bf16[2048,2048]{1,0:T(8,128)(2,1)} %param.23, s32[]{:T(128)S(6)} %select_n.90), kind=kOutput, calls=%fused_computation.33 | convolution fusion | flops 1074790400 | bytes 4718596 | tf_op jit(solution)/shard_map/dot_general | solution.py:149
  83.7 0.7 copy.43
  84.4 3.3 all-gather.3.cloned.1.call-done
  87.7 56.5 %all-gather.5.cloned.1.call-done = bf16[8192,512]{0,1:T(8,128)(2,1)} async-done(((bf16[1024,512]{0,1:T(8,128)(2,1)}), bf16[8192,512]{0,1:T(8,128)(2,1)}) %all-gather.5.cloned.1.call-update) | async-done | bytes 8388624 | tf_op jit(solution)/shard_map/all_gather | solution.py:50
  144.1 1.4 broadcast_in_dim.90
  145.6 144.4 %while.18 = (s32[]{:T(128)}, f32[4,1024,128]{2,1,0:T(8,128)}, f32[4,1024]{1,0:T(4,128)S(1)}, f32[4,1024]{1,0:T(4,128)S(1)}, s32[]{:T(128)}, /*index=5*/bf16[8192...) while((s32[]{:T(128)}, f32[4,1024,128]{2,1,0:T(8,128)}, ...), condition=%wide.region_6.7_spmd.clone, body=%wide.region_1.6_spmd.clone.sunk | while | flops 2204116992 | bytes 66347328 | solution.py:69
  146.2 19.9 %conditional.3 = ((f32[4,1024,128]{2,1,0:T(8,128)}, f32[4,1024]{1,0:T(4,128)S(1)}, f32[4,1024]{1,0:T(4,128)S(1)})) conditional(s32[]{:T(128)} %convert_element_type.75, (f32[4,1024,128]{2,1,0:T(8,128)}, f32[4,1024]{1,0:T(4,128)S(1)}, f32[4,1024]{1,0:T(4,128)S(1)}) %tuple.66, (s32[]{:T(128)}, s32[]{:T(128)}, bf16[8192,512]{0,1:T(8,128)(2,1)}, ...), branch_computations={%region_2.0_spmd, %region_3.5_spmd} | conditional | flops 2204116992 | bytes 66342992 | solution.py:67
  146.3 2.7 constant_dynamic-slice_fusion
  149.6 3.6 fusion.2
  153.2 4.2 %fusion.3 = f32[4,1024]{1,0:T(4,128)S(1)} fusion(f32[4,1024,1024]{2,1,0:T(8,128)S(1)} %get-tuple-element.341, f32[4,1024]{1,0:T(4,128)S(1)} %max.5, pred[1024,1024]{0,1:T(8,128)(4,1)S(1)} %broadcast_compare_fusion), kind=kLoop, calls=%fused_computation.6 | loop fusion | flops 20967424 | bytes 17858560 | tf_op jit(solution)/shard_map/while/body/eval_jaxpr/cond/branch_1_fun/reduce_sum | solution.py:29
  157.5 8.6 %multiply_add_fusion = f32[4,1024,128]{2,1,0:T(8,128)} fusion(f32[4,1024,128]{2,1,0:T(8,128)} %get-tuple-element.245, bf16[1024,4,128]{0,2,1:T(8,128)(2,1)} %bitcast.72, f32[4,1024,1024]{2,1,0:T(8,128)S(1)} %get-tuple-element.341, f32[4,1024]{1,0:T(4,128)S(1)} %max.5, pred[1024,1024]{0,1:T(8,128)(4,1)S(1)} %broadcast_compare_fusion, ...), kind=kOutput, calls=%fused_computation.10 | convolution fusion | flops 1095761920 | bytes 23101440 | tf_op jit(solution)/shard_map/while/body/eval_jaxpr/cond/branch_1_fun/hqk,khd->hqd/dot_general | solution.py:30
  166.8 19.9 %conditional.3 = ((f32[4,1024,128]{2,1,0:T(8,128)}, f32[4,1024]{1,0:T(4,128)S(1)}, f32[4,1024]{1,0:T(4,128)S(1)})) conditional(s32[]{:T(128)} %convert_element_type.75, (f32[4,1024,128]{2,1,0:T(8,128)}, f32[4,1024]{1,0:T(4,128)S(1)}, f32[4,1024]{1,0:T(4,128)S(1)}) %tuple.66, (s32[]{:T(128)}, s32[]{:T(128)}, bf16[8192,512]{0,1:T(8,128)(2,1)}, ...), branch_computations={%region_2.0_spmd, %region_3.5_spmd} | conditional | flops 2204116992 | bytes 66342992 | solution.py:67
  166.8 2.7 constant_dynamic-slice_fusion
  169.5 0.7 broadcast_compare_fusion
  170.1 3.6 fusion.2
  173.8 4.2 %fusion.3 = f32[4,1024]{1,0:T(4,128)S(1)} fusion(f32[4,1024,1024]{2,1,0:T(8,128)S(1)} %get-tuple-element.341, f32[4,1024]{1,0:T(4,128)S(1)} %max.5, pred[1024,1024]{0,1:T(8,128)(4,1)S(1)} %broadcast_compare_fusion), kind=kLoop, calls=%fused_computation.6 | loop fusion | flops 20967424 | bytes 17858560 | tf_op jit(solution)/shard_map/while/body/eval_jaxpr/cond/branch_1_fun/reduce_sum | solution.py:29
  178.0 8.6 %multiply_add_fusion = f32[4,1024,128]{2,1,0:T(8,128)} fusion(f32[4,1024,128]{2,1,0:T(8,128)} %get-tuple-element.245, bf16[1024,4,128]{0,2,1:T(8,128)(2,1)} %bitcast.72, f32[4,1024,1024]{2,1,0:T(8,128)S(1)} %get-tuple-element.341, f32[4,1024]{1,0:T(4,128)S(1)} %max.5, pred[1024,1024]{0,1:T(8,128)(4,1)S(1)} %broadcast_compare_fusion, ...), kind=kOutput, calls=%fused_computation.10 | convolution fusion | flops 1095761920 | bytes 23101440 | tf_op jit(solution)/shard_map/while/body/eval_jaxpr/cond/branch_1_fun/hqk,khd->hqd/dot_general | solution.py:30
  187.3 19.9 %conditional.3 = ((f32[4,1024,128]{2,1,0:T(8,128)}, f32[4,1024]{1,0:T(4,128)S(1)}, f32[4,1024]{1,0:T(4,128)S(1)})) conditional(s32[]{:T(128)} %convert_element_type.75, (f32[4,1024,128]{2,1,0:T(8,128)}, f32[4,1024]{1,0:T(4,128)S(1)}, f32[4,1024]{1,0:T(4,128)S(1)}) %tuple.66, (s32[]{:T(128)}, s32[]{:T(128)}, bf16[8192,512]{0,1:T(8,128)(2,1)}, ...), branch_computations={%region_2.0_spmd, %region_3.5_spmd} | conditional | flops 2204116992 | bytes 66342992 | solution.py:67
  187.3 2.7 constant_dynamic-slice_fusion
  190.0 0.7 broadcast_compare_fusion
  190.7 3.6 fusion.2
  194.3 4.2 %fusion.3 = f32[4,1024]{1,0:T(4,128)S(1)} fusion(f32[4,1024,1024]{2,1,0:T(8,128)S(1)} %get-tuple-element.341, f32[4,1024]{1,0:T(4,128)S(1)} %max.5, pred[1024,1024]{0,1:T(8,128)(4,1)S(1)} %broadcast_compare_fusion), kind=kLoop, calls=%fused_computation.6 | loop fusion | flops 20967424 | bytes 17858560 | tf_op jit(solution)/shard_map/while/body/eval_jaxpr/cond/branch_1_fun/reduce_sum | solution.py:29
  198.5 8.6 %multiply_add_fusion = f32[4,1024,128]{2,1,0:T(8,128)} fusion(f32[4,1024,128]{2,1,0:T(8,128)} %get-tuple-element.245, bf16[1024,4,128]{0,2,1:T(8,128)(2,1)} %bitcast.72, f32[4,1024,1024]{2,1,0:T(8,128)S(1)} %get-tuple-element.341, f32[4,1024]{1,0:T(4,128)S(1)} %max.5, pred[1024,1024]{0,1:T(8,128)(4,1)S(1)} %broadcast_compare_fusion, ...), kind=kOutput, calls=%fused_computation.10 | convolution fusion | flops 1095761920 | bytes 23101440 | tf_op jit(solution)/shard_map/while/body/eval_jaxpr/cond/branch_1_fun/hqk,khd->hqd/dot_general | solution.py:30
  207.8 19.9 %conditional.3 = ((f32[4,1024,128]{2,1,0:T(8,128)}, f32[4,1024]{1,0:T(4,128)S(1)}, f32[4,1024]{1,0:T(4,128)S(1)})) conditional(s32[]{:T(128)} %convert_element_type.75, (f32[4,1024,128]{2,1,0:T(8,128)}, f32[4,1024]{1,0:T(4,128)S(1)}, f32[4,1024]{1,0:T(4,128)S(1)}) %tuple.66, (s32[]{:T(128)}, s32[]{:T(128)}, bf16[8192,512]{0,1:T(8,128)(2,1)}, ...), branch_computations={%region_2.0_spmd, %region_3.5_spmd} | conditional | flops 2204116992 | bytes 66342992 | solution.py:67
  207.8 2.7 constant_dynamic-slice_fusion
  210.5 0.7 broadcast_compare_fusion
  211.2 3.6 fusion.2
  214.8 4.2 %fusion.3 = f32[4,1024]{1,0:T(4,128)S(1)} fusion(f32[4,1024,1024]{2,1,0:T(8,128)S(1)} %get-tuple-element.341, f32[4,1024]{1,0:T(4,128)S(1)} %max.5, pred[1024,1024]{0,1:T(8,128)(4,1)S(1)} %broadcast_compare_fusion), kind=kLoop, calls=%fused_computation.6 | loop fusion | flops 20967424 | bytes 17858560 | tf_op jit(solution)/shard_map/while/body/eval_jaxpr/cond/branch_1_fun/reduce_sum | solution.py:29
  219.1 8.6 %multiply_add_fusion = f32[4,1024,128]{2,1,0:T(8,128)} fusion(f32[4,1024,128]{2,1,0:T(8,128)} %get-tuple-element.245, bf16[1024,4,128]{0,2,1:T(8,128)(2,1)} %bitcast.72, f32[4,1024,1024]{2,1,0:T(8,128)S(1)} %get-tuple-element.341, f32[4,1024]{1,0:T(4,128)S(1)} %max.5, pred[1024,1024]{0,1:T(8,128)(4,1)S(1)} %broadcast_compare_fusion, ...), kind=kOutput, calls=%fused_computation.10 | convolution fusion | flops 1095761920 | bytes 23101440 | tf_op jit(solution)/shard_map/while/body/eval_jaxpr/cond/branch_1_fun/hqk,khd->hqd/dot_general | solution.py:30
  228.3 19.9 %conditional.3 = ((f32[4,1024,128]{2,1,0:T(8,128)}, f32[4,1024]{1,0:T(4,128)S(1)}, f32[4,1024]{1,0:T(4,128)S(1)})) conditional(s32[]{:T(128)} %convert_element_type.75, (f32[4,1024,128]{2,1,0:T(8,128)}, f32[4,1024]{1,0:T(4,128)S(1)}, f32[4,1024]{1,0:T(4,128)S(1)}) %tuple.66, (s32[]{:T(128)}, s32[]{:T(128)}, bf16[8192,512]{0,1:T(8,128)(2,1)}, ...), branch_computations={%region_2.0_spmd, %region_3.5_spmd} | conditional | flops 2204116992 | bytes 66342992 | solution.py:67
  228.4 2.7 constant_dynamic-slice_fusion
  231.1 0.7 broadcast_compare_fusion
  231.7 3.6 fusion.2
  235.3 4.2 %fusion.3 = f32[4,1024]{1,0:T(4,128)S(1)} fusion(f32[4,1024,1024]{2,1,0:T(8,128)S(1)} %get-tuple-element.341, f32[4,1024]{1,0:T(4,128)S(1)} %max.5, pred[1024,1024]{0,1:T(8,128)(4,1)S(1)} %broadcast_compare_fusion), kind=kLoop, calls=%fused_computation.6 | loop fusion | flops 20967424 | bytes 17858560 | tf_op jit(solution)/shard_map/while/body/eval_jaxpr/cond/branch_1_fun/reduce_sum | solution.py:29
  239.6 8.6 %multiply_add_fusion = f32[4,1024,128]{2,1,0:T(8,128)} fusion(f32[4,1024,128]{2,1,0:T(8,128)} %get-tuple-element.245, bf16[1024,4,128]{0,2,1:T(8,128)(2,1)} %bitcast.72, f32[4,1024,1024]{2,1,0:T(8,128)S(1)} %get-tuple-element.341, f32[4,1024]{1,0:T(4,128)S(1)} %max.5, pred[1024,1024]{0,1:T(8,128)(4,1)S(1)} %broadcast_compare_fusion, ...), kind=kOutput, calls=%fused_computation.10 | convolution fusion | flops 1095761920 | bytes 23101440 | tf_op jit(solution)/shard_map/while/body/eval_jaxpr/cond/branch_1_fun/hqk,khd->hqd/dot_general | solution.py:30
  248.9 19.9 %conditional.3 = ((f32[4,1024,128]{2,1,0:T(8,128)}, f32[4,1024]{1,0:T(4,128)S(1)}, f32[4,1024]{1,0:T(4,128)S(1)})) conditional(s32[]{:T(128)} %convert_element_type.75, (f32[4,1024,128]{2,1,0:T(8,128)}, f32[4,1024]{1,0:T(4,128)S(1)}, f32[4,1024]{1,0:T(4,128)S(1)}) %tuple.66, (s32[]{:T(128)}, s32[]{:T(128)}, bf16[8192,512]{0,1:T(8,128)(2,1)}, ...), branch_computations={%region_2.0_spmd, %region_3.5_spmd} | conditional | flops 2204116992 | bytes 66342992 | solution.py:67
  248.9 2.7 constant_dynamic-slice_fusion
  251.6 0.7 broadcast_compare_fusion
  252.2 3.6 fusion.2
  255.9 4.2 %fusion.3 = f32[4,1024]{1,0:T(4,128)S(1)} fusion(f32[4,1024,1024]{2,1,0:T(8,128)S(1)} %get-tuple-element.341, f32[4,1024]{1,0:T(4,128)S(1)} %max.5, pred[1024,1024]{0,1:T(8,128)(4,1)S(1)} %broadcast_compare_fusion), kind=kLoop, calls=%fused_computation.6 | loop fusion | flops 20967424 | bytes 17858560 | tf_op jit(solution)/shard_map/while/body/eval_jaxpr/cond/branch_1_fun/reduce_sum | solution.py:29
  260.1 8.6 %multiply_add_fusion = f32[4,1024,128]{2,1,0:T(8,128)} fusion(f32[4,1024,128]{2,1,0:T(8,128)} %get-tuple-element.245, bf16[1024,4,128]{0,2,1:T(8,128)(2,1)} %bitcast.72, f32[4,1024,1024]{2,1,0:T(8,128)S(1)} %get-tuple-element.341, f32[4,1024]{1,0:T(4,128)S(1)} %max.5, pred[1024,1024]{0,1:T(8,128)(4,1)S(1)} %broadcast_compare_fusion, ...), kind=kOutput, calls=%fused_computation.10 | convolution fusion | flops 1095761920 | bytes 23101440 | tf_op jit(solution)/shard_map/while/body/eval_jaxpr/cond/branch_1_fun/hqk,khd->hqd/dot_general | solution.py:30
  269.4 19.9 %conditional.3 = ((f32[4,1024,128]{2,1,0:T(8,128)}, f32[4,1024]{1,0:T(4,128)S(1)}, f32[4,1024]{1,0:T(4,128)S(1)})) conditional(s32[]{:T(128)} %convert_element_type.75, (f32[4,1024,128]{2,1,0:T(8,128)}, f32[4,1024]{1,0:T(4,128)S(1)}, f32[4,1024]{1,0:T(4,128)S(1)}) %tuple.66, (s32[]{:T(128)}, s32[]{:T(128)}, bf16[8192,512]{0,1:T(8,128)(2,1)}, ...), branch_computations={%region_2.0_spmd, %region_3.5_spmd} | conditional | flops 2204116992 | bytes 66342992 | solution.py:67
  269.4 2.7 constant_dynamic-slice_fusion
  272.1 0.7 broadcast_compare_fusion
  272.8 3.6 fusion.2
  276.4 4.2 %fusion.3 = f32[4,1024]{1,0:T(4,128)S(1)} fusion(f32[4,1024,1024]{2,1,0:T(8,128)S(1)} %get-tuple-element.341, f32[4,1024]{1,0:T(4,128)S(1)} %max.5, pred[1024,1024]{0,1:T(8,128)(4,1)S(1)} %broadcast_compare_fusion), kind=kLoop, calls=%fused_computation.6 | loop fusion | flops 20967424 | bytes 17858560 | tf_op jit(solution)/shard_map/while/body/eval_jaxpr/cond/branch_1_fun/reduce_sum | solution.py:29
  280.6 8.6 %multiply_add_fusion = f32[4,1024,128]{2,1,0:T(8,128)} fusion(f32[4,1024,128]{2,1,0:T(8,128)} %get-tuple-element.245, bf16[1024,4,128]{0,2,1:T(8,128)(2,1)} %bitcast.72, f32[4,1024,1024]{2,1,0:T(8,128)S(1)} %get-tuple-element.341, f32[4,1024]{1,0:T(4,128)S(1)} %max.5, pred[1024,1024]{0,1:T(8,128)(4,1)S(1)} %broadcast_compare_fusion, ...), kind=kOutput, calls=%fused_computation.10 | convolution fusion | flops 1095761920 | bytes 23101440 | tf_op jit(solution)/shard_map/while/body/eval_jaxpr/cond/branch_1_fun/hqk,khd->hqd/dot_general | solution.py:30
  290.0 1.9 copy.44
  292.2 6.1 %convolution_convert_fusion = bf16[1024,2048]{1,0:T(8,128)(2,1)} fusion(bf16[1024,512]{0,1:T(8,128)(2,1)S(1)} %bitcast.77, bf16[2048,2048]{1,0:T(8,128)(2,1)} %param.23, s32[]{:T(128)S(6)} %select_n.90), kind=kOutput, calls=%fused_computation.30 | convolution fusion | flops 2149580800 | bytes 7340036 | tf_op jit(solution)/shard_map/dot_general | solution.py:143
  298.3 97.4 %reduce-scatter.3.cloned.1.call-done = bf16[256,2048]{1,0:T(8,128)(2,1)} async-done(((bf16[1024,2048]{1,0:T(8,128)(2,1)}), bf16[256,2048]{1,0:T(8,128)(2,1)}) %reduce-scatter.3.cloned.1.call-update) | async-done | bytes 1048592 | tf_op jit(solution)/shard_map/reduce_scatter | solution.py:142
  (90 shorter events, 4.7 us)
Async XLA Ops:
  8.0 5.7 %copy-start = (bf16[64,2,16,512]{3,2,1,0:T(8,128)(2,1)S(1)}, bf16[64,2,16,512]{3,2,1,0:T(8,128)(2,1)}, u32[]{:S(2)}) copy-start(bf16[64,2,16,512]{3,2,1,0:T(8,128)(2,1)} %param.21) | copy-start | bytes 6291460
  8.0 4.9 %copy-start.6 = (s32[8,16,4]{1,2,0:T(4,128)S(1)}, s32[8,16,4]{1,2,0:T(4,128)}, u32[]{:S(2)}) copy-start(s32[8,16,4]{1,2,0:T(4,128)} %param.22) | copy-start | bytes 6148
  8.0 79.6 %all-gather.3.cloned.1.call-start = ((), (), s32[]{:S(2)}) async-start(), calls=%async_computation.3 | async-start | bytes 9437184 | tf_op jit(solution)/shard_map/all_gather | solution.py:49
  10.5 9.4 %copy-start.4 = (bf16[512,512]{1,0:T(8,128)(2,1)S(1)}, bf16[512,512]{1,0:T(8,128)(2,1)}, u32[]{:S(2)}) copy-start(bf16[512,512]{1,0:T(8,128)(2,1)} %param.18) | copy-start | bytes 1572868
  10.5 133.6 %all-gather.5.cloned.1.call-start = ((), (), s32[]{:S(2)}) async-start(), calls=%async_computation.4 | async-start | bytes 9437184 | tf_op jit(solution)/shard_map/all_gather | solution.py:50
  12.9 10.5 %copy-start.8 = (s32[1,512]{1,0:T(1,128)S(1)}, s32[1,512]{1,0:T(1,128)}, u32[]{:S(2)}) copy-start(s32[1,512]{1,0:T(1,128)} %param.20) | copy-start | bytes 6148
  12.9 10.6 %copy-start.7 = (s32[1536]{0:T(1024)S(1)}, s32[1536]{0:T(1024)}, u32[]{:S(2)}) copy-start(s32[1536]{0:T(1024)} %constant.138.clone.1) | copy-start | bytes 18436
  15.7 39.7 %all-to-all-start = ((bf16[8,8,2,16,512]{4,3,2,1,0:T(8,128)(2,1)}), bf16[8,8,2,16,512]{4,3,2,1,0:T(8,128)(2,1)S(1)}, u32[]{:S(2)}, u32[]{:S(2)}) async-start(bf16[8,8,2,16,512]{4,3,2,1,0:T(8,128)(2,1)} %bitcast.74), calls=%async_computation.1 | async-start | bytes 4194304 | tf_op jit(solution)/shard_map/all_to_all | solution.py:93
  19.9 278.4 %reduce-scatter.5.cloned.1.call-start = ((), (), s32[]{:S(2)}) async-start(), calls=%async_computation.6 | async-start | bytes 2621440 | tf_op jit(solution)/shard_map/reduce_scatter | solution.py:148
  64.4 9.6 %copy-start.3 = (bf16[1024,4,128]{0,2,1:T(8,128)(2,1)S(1)}, bf16[1024,4,128]{0,2,1:T(8,128)(2,1)}, u32[]{:S(2)}) copy-start(bf16[1024,4,128]{0,2,1:T(8,128)(2,1)} %copy.55) | copy-start | bytes 3145732
  64.4 9.6 %copy-start.5 = (bf16[512,512]{0,1:T(8,128)(2,1)S(1)}, bf16[512,512]{0,1:T(8,128)(2,1)}, u32[]{:S(2)}) copy-start(bf16[512,512]{0,1:T(8,128)(2,1)} %copy.54) | copy-start | bytes 1572868
  77.9 5.2 %copy-start.2 = (bf16[1024,512]{1,0:T(8,128)(2,1)S(1)}, bf16[1024,512]{1,0:T(8,128)(2,1)}, u32[]{:S(2)}) copy-start(bf16[1024,512]{1,0:T(8,128)(2,1)} %param.14) | copy-start | bytes 3145732
  82.3 313.4 %reduce-scatter.3.cloned.1.call-start = ((), (), s32[]{:S(2)}) async-start(), calls=%async_computation.5 | async-start | bytes 5242880 | tf_op jit(solution)/shard_map/reduce_scatter | solution.py:142
  292.2 103.5 %copy-start.1 = (bf16[64,2,16,512]{3,2,1,0:T(8,128)(2,1)S(1)}, bf16[64,2,16,512]{3,2,1,0:T(8,128)(2,1)}, u32[]{:S(2)}) copy-start(bf16[64,2,16,512]{3,2,1,0:T(8,128)(2,1)} %param.21) | copy-start | bytes 6291460
Sparse Core Ops, SparseCore 0:
  11.5 76.1 all-gather.2
  89.7 54.3 all-gather.4
Sparse Core Ops, SparseCore 1:
  82.4 43.9 reduce-scatter.4
  298.4 97.3 reduce-scatter.2
where the time goes:
time: 406 us; the launch traced here: 403 us
  waiting for transfers between devices  187 us (46%)
  matrix products  103 us (25%)
  other arithmetic  47.3 us (12%)
  local copies, waits for them, and re-layouts  39.7 us (10%)
  between operations  15.7 us (4%)
  loops' own time  5.59 us (1%)
  starting transfers between devices  4.5 us (1%)
    reduce_scatter x1, waiting for transfers between devices, per_device(): lax.psum_scatter(jnp.dot(long_attn, w_rows, preferred_element_type=jnp.fl...  97.4 us
    dot_general x7, matrix products, fold_block(): jnp.einsum('hqk,khd->hqd', weights.astype(jnp.bfloat16), value_heads, pre...  60.5 us
    all_gather x1, waiting for transfers between devices, prompt_attention(): value_piece = lax.all_gather(long_v, 'blk', axis=0, tiled=True)  56.5 us
    all_to_all x1, waiting for transfers between devices, pack_attention(): lax.all_to_all(outgoing, 'blk', split_axis=0, concat_axis=0, tiled=True)  30 us
    reduce_sum x7, other arithmetic, fold_block(): run_total = run_total * factor + jnp.sum(weights, axis=-1)  29.3 us
    dot_general x7, matrix products, fold_block(): jnp.einsum('qhd,khd->hqk', query_heads, key_heads, preferred_element_type...  25.2 us
    dynamic_slice x7, local copies, waits for them, and re-layouts, one_step(): lax.dynamic_slice_in_dim(value_piece, block_start, step_rows, 0)  18.8 us
    sub x1, other arithmetic, pack_attention(): weights = jnp.where(allowed, jnp.exp(scores - row_max[..., None]), 0.0)  9.6 us
  transfers between devices with their start and end apart: 5, of which 4 were waited for; matrix products, arithmetic and copies ran while one was open for 47% of the time, Pallas kernels for 0%

commit v1 on v0

v1 whole, which is shorter than its diff:
```python
import functools

import jax
import jax.numpy as jnp
from jax import lax
from jax.experimental import pallas as pl
from jax.experimental.pallas import tpu as pltpu
from jax.sharding import PartitionSpec as P

HD = 128
PPS = 4
EXP2_SCALE = HD ** -0.5 * 1.4426950408889634
VERY_NEGATIVE = -1e30
MESH = pl.DeviceIdType.MESH


def lane_sum(x):
    total = x[:, :128]
    for at in range(128, x.shape[1], 128):
        total = total + x[:, at:at + 128]
    return total


def scores_of(q, k):
    return lax.dot_general(q, k, (((1,), (1,)), ((), ())), preferred_element_type=jnp.float32)


def kernel(N, RN, H, G, long_q, long_k, long_v, pages_out, sq, sk, sv, q_seg, k_seg,
           l_out, s_out, kbuf, vbuf, qbuf, obuf, pbuf, sbuf,
           kv_send, kv_recv, fwd_send, q_send, q_recv, p_send, p_recv,
           o_send, o_recv, s_send, s_recv):
    d = lax.axis_index("blk")
    req = lax.axis_index("req")
    c, p = d // G, d % G
    R = kbuf.shape[1]
    rr = R // RN
    srows = sbuf.shape[0] // RN
    m_d = (c % 2) * (G - 1 - 2 * p) + p
    total = N * RN
    me = d * RN + req

    barrier = pltpu.get_barrier_semaphore()

    @pl.loop(1, total)
    def _(k):
        other = (me + k) % total
        pl.semaphore_signal(barrier, inc=1, device_id=(other // RN, other % RN), device_id_type=MESH)

    pl.semaphore_wait(barrier, total - 1)

    def head_cols(h):
        return pl.ds(pl.multiple_of(h * HD, HD), HD)

    def kv_copy(k, which):
        h = (c + k) % H
        src = (long_k, long_v)[which].at[:, head_cols(h)]
        dst = (kbuf, vbuf)[which].at[d]
        if k == 0:
            return pltpu.make_async_copy(src, dst, kv_recv.at[which, d])
        return pltpu.make_async_remote_copy(
            src, dst, kv_send.at[which, k], kv_recv.at[which, d],
            device_id=(h * G + p, req), device_id_type=MESH)

    def q_copy(k):
        h = (c + k) % H
        return pltpu.make_async_remote_copy(
            long_q.at[:, head_cols(h)], qbuf.at[c], q_send.at[k], q_recv.at[c],
            device_id=(h * G + m_d, req), device_id_type=MESH)

    q_stays = m_d == p

    for k in list(range(1, H)) + [0]:
        kv_copy(k, 0).start()
        if k == 0:
            @pl.when(q_stays)
            def _():
                pltpu.make_async_copy(long_q.at[:, head_cols(c)], qbuf.at[c], q_recv.at[c]).start()

            @pl.when(jnp.logical_not(q_stays))
            def _():
                q_copy(0).start()
        else:
            q_copy(k).start()
        kv_copy(k, 1).start()

    def page_copy(k):
        other = (d + k) % N
        if k == 0:
            return pltpu.make_async_copy(pages_out.at[d], pbuf.at[d], p_recv.at[d])
        return pltpu.make_async_remote_copy(
            pages_out.at[other], pbuf.at[d], p_send.at[k], p_recv.at[d],
            device_id=(other, req), device_id_type=MESH)

    for k in range(N):
        page_copy(k).start()

    def arrived(buf, b, sem):
        pltpu.make_async_copy(buf.at[b], buf.at[b], sem).wait()

    def fwd_copy(j, k, which):
        buf = (kbuf, vbuf)[which]
        b = j * G + p
        return pltpu.make_async_remote_copy(
            buf.at[b], buf.at[b], fwd_send.at[which, j, k], kv_recv.at[which, b],
            device_id=(c * G + (p + k) % G, req), device_id_type=MESH)

    def out_copy(j, b, r):
        dst = l_out.at[:, head_cols(req * H + c)]
        return pltpu.make_async_remote_copy(
            obuf.at[j, pl.ds(r * rr, rr)], dst, o_send.at[j, r], o_recv.at[req * H + c],
            device_id=(b, r), device_id_type=MESH)

    tq = min(256, R)

    def step(state, q, k, v, mask):
        m, l, acc = state
        s = scores_of(q, k)
        if mask is not None:
            s = jnp.where(mask, s, VERY_NEGATIVE)
        new = jnp.maximum(m, jnp.max(s, axis=1, keepdims=True))
        w = jnp.exp2((s - new) * EXP2_SCALE)
        f = jnp.exp2((m - new) * EXP2_SCALE)
        l = l * f + lane_sum(w)
        acc = acc * f + jnp.dot(w.astype(jnp.bfloat16), v, preferred_element_type=jnp.float32)
        return new, l, acc

    def empty(rows):
        return (jnp.full((rows, 1), VERY_NEGATIVE, jnp.float32),
                jnp.zeros((rows, HD), jnp.float32), jnp.zeros((rows, HD), jnp.float32))

    def finish(state):
        return (state[2] / jnp.sum(state[1], axis=1, keepdims=True)).astype(jnp.bfloat16)

    def block_of(j):
        return j * G + (j % 2) * (G - 1 - 2 * p) + p

    @pl.loop(0, H)
    def _(j):
        b = block_of(j)
        mine = j * G + p
        for which, buf in ((0, kbuf), (1, vbuf)):
            arrived(buf, mine, kv_recv.at[which, mine])
            for k in range(1, G):
                fwd_copy(j, k, which).start()
        for k in range(1, G):
            theirs = j * G + (p + k) % G
            for which, buf in ((0, kbuf), (1, vbuf)):
                arrived(buf, theirs, kv_recv.at[which, theirs])
        arrived(qbuf, j, q_recv.at[j])
        for t in range(R // tq):
            rows = pl.ds(t * tq, tq)
            q = qbuf[j, rows, :]
            keys = (t + 1) * tq
            mask = (lax.broadcasted_iota(jnp.int32, (tq, keys), 1)
                    <= lax.broadcasted_iota(jnp.int32, (tq, keys), 0) + t * tq)
            state = step(empty(tq), q, kbuf[b, pl.ds(0, keys), :], vbuf[b, pl.ds(0, keys), :], mask)
            state = lax.fori_loop(
                0, b, lambda i, st: step(st, q, kbuf[i], vbuf[i], None), state)
            obuf[j, rows, :] = finish(state)
        for r in range(RN):
            here = jnp.logical_and(b == d, req == r)

            @pl.when(here)
            def _():
                pltpu.make_async_copy(
                    obuf.at[j, pl.ds(r * rr, rr)], l_out.at[:, head_cols(req * H + c)],
                    o_recv.at[req * H + c]).start()

            @pl.when(jnp.logical_not(here))
            def _():
                out_copy(j, b, r).start()

    for k in range(N):
        arrived(pbuf, (d + k) % N, p_recv.at[(d + k) % N])

    cache_len = k_seg.shape[1] - sk.shape[0]
    pack = sbuf.shape[0]
    ts = min(256, pack)

    @pl.loop(0, H)
    def _(h):
        cols = head_cols(h)
        ck = pbuf[:, :, 0, :, cols].reshape(cache_len, HD)
        cv = pbuf[:, :, 1, :, cols].reshape(cache_len, HD)
        for t in range(pack // ts):
            rows = pl.ds(t * ts, ts)
            keys = (t + 1) * ts
            q = sq[rows, cols]
            seg = q_seg[rows, :]
            own = jnp.logical_and(
                k_seg[:, pl.ds(cache_len, keys)] == seg,
                lax.broadcasted_iota(jnp.int32, (ts, keys), 1)
                <= lax.broadcasted_iota(jnp.int32, (ts, keys), 0) + t * ts)
            state = step(empty(ts), q, sk[pl.ds(0, keys), cols], sv[pl.ds(0, keys), cols], own)
            state = step(state, q, ck, cv, k_seg[:, pl.ds(0, cache_len)] == seg)
            sbuf[rows, cols] = finish(state)

    def short_copy(k):
        r = (req + k) % RN
        W = sbuf.shape[1]
        src = sbuf.at[pl.ds(pl.multiple_of(r * srows, srows), srows)]
        dst = s_out.at[:, pl.ds(pl.multiple_of(req * W, W), W)]
        if k == 0:
            return pltpu.make_async_copy(src, dst, s_recv.at[req])
        return pltpu.make_async_remote_copy(
            src, dst, s_send.at[k], s_recv.at[req], device_id=(d, r), device_id_type=MESH)

    for k in range(RN):
        short_copy(k).start()
    for k in range(RN):
        r = (req + k) % RN
        W = sbuf.shape[1]
        dst = s_out.at[:, pl.ds(pl.multiple_of(r * W, W), W)]
        pltpu.make_async_copy(dst, dst, s_recv.at[r]).wait()

    @pl.loop(0, RN * H)
    def _(i):
        dst = l_out.at[:, head_cols(i)]
        pltpu.make_async_copy(dst, dst, o_recv.at[i]).wait()

    for k in range(1, RN):
        short_copy(k).wait_send()
    for k in range(1, N):
        page_copy(k).wait_send()
    for k in range(1, H):
        kv_copy(k, 0).wait_send()
        kv_copy(k, 1).wait_send()
        q_copy(k).wait_send()

    @pl.when(jnp.logical_not(q_stays))
    def _():
        q_copy(0).wait_send()

    @pl.loop(0, H)
    def _(j):
        b = block_of(j)
        for k in range(1, G):
            fwd_copy(j, k, 0).wait_send()
            fwd_copy(j, k, 1).wait_send()
        for r in range(RN):
            @pl.when(jnp.logical_not(jnp.logical_and(b == d, req == r)))
            def _():
                out_copy(j, b, r).wait_send()


def per_device(
    long_q, long_k, long_v, short_q, short_k, short_v, short_seg, pool_kv, page_table, w_out
):
    N = lax.axis_size("blk")
    RN = lax.axis_size("req")
    d = lax.axis_index("blk")
    R, W = long_q.shape
    H = W // HD
    G = N // H
    pack = short_q.shape[0]
    pool_pages = pool_kv.shape[0]
    page_len = pool_kv.shape[2]
    table = page_table.reshape(N, -1)
    entries = table.shape[1]
    cap = entries // N
    owners = table // pool_pages
    places = table % pool_pages
    wanted = owners == d
    ranks = jnp.cumsum(wanted.astype(jnp.int32), axis=1) - 1
    picked = wanted[:, :, None] & (
        ranks[:, :, None] == jnp.arange(cap, dtype=jnp.int32)[None, None, :]
    )
    send_places = jnp.sum(jnp.where(picked, places[:, :, None], 0), axis=1)
    outgoing = pool_kv[send_places.reshape(-1)].reshape(N, cap, 2, page_len, W)
    my_owners = lax.dynamic_index_in_dim(owners, d, 0, keepdims=False)
    order = jnp.arange(entries, dtype=jnp.int32)
    before = (my_owners[None, :] == my_owners[:, None]) & (order[None, :] < order[:, None])
    slots = my_owners * cap + jnp.sum(before.astype(jnp.int32), axis=1)
    slot_seg = jnp.sum(jnp.where(slots[:, None] == order[None, :], (order // PPS)[:, None], 0), axis=0)
    segment = short_seg[0]
    k_seg = jnp.concatenate([jnp.repeat(slot_seg, page_len), segment])[None, :]
    q_seg = segment[:, None]

    DMA = pltpu.SemaphoreType.DMA
    vmem = pl.BlockSpec(memory_space=pltpu.VMEM)
    anywhere = pl.BlockSpec(memory_space=pl.ANY)
    bf16 = jnp.bfloat16
    l_attn, s_attn = pl.pallas_call(
        functools.partial(kernel, N, RN, H, G),
        out_shape=(jax.ShapeDtypeStruct((R // RN, W * RN), bf16),
                   jax.ShapeDtypeStruct((pack // RN, W * RN), bf16)),
        in_specs=[anywhere] * 4 + [vmem] * 5,
        out_specs=(anywhere, anywhere),
        scratch_shapes=[
            pltpu.VMEM((N, R, HD), bf16), pltpu.VMEM((N, R, HD), bf16),
            pltpu.VMEM((H, R, HD), bf16), pltpu.VMEM((H, R, HD), bf16),
            pltpu.VMEM((N, cap, 2, page_len, W), bf16), pltpu.VMEM((pack, W), bf16),
            DMA((2, H)), DMA((2, N)), DMA((2, H, G)), DMA((H,)), DMA((H,)),
            DMA((N,)), DMA((N,)), DMA((H, RN)), DMA((RN * H,)), DMA((RN,)), DMA((RN,)),
        ],
        compiler_params=pltpu.CompilerParams(
            collective_id=0, has_side_effects=True, vmem_limit_bytes=52 * 2**20),
    )(long_q, long_k, long_v, outgoing, short_q, short_k, short_v, q_seg, k_seg)
    return (jnp.dot(l_attn, w_out, preferred_element_type=jnp.float32).astype(bf16),
            jnp.dot(s_attn, w_out, preferred_element_type=jnp.float32).astype(bf16))


def solution(mesh):
    placed = (
        P("blk", "req"),
        P("blk", "req"),
        P("blk", "req"),
        P("blk", "req"),
        P("blk", "req"),
        P("blk", "req"),
        P("blk", None),
        P("blk", None, None, "req"),
        P(),
        P(),
    )
    return jax.shard_map(
        per_device,
        mesh=mesh,
        in_specs=placed,
        out_specs=(P(("blk", "req"), None), P(("blk", "req"), None)),
        check_vma=False,
    )
```

time: 406 us -> 135 us (0.33)
  waiting for transfers between devices: 187 us -> 0 us
  Pallas kernels: 0 us -> 117 us
  matrix products: 103 us -> 9.2 us
  other arithmetic: 47.3 us -> 1.46 us
  local copies, waits for them, and re-layouts: 39.7 us -> 6.2 us
  between operations: 15.7 us -> 0.72 us
  loops' own time: 5.59 us -> 0 us
  starting transfers between devices: 4.5 us -> 0 us
    pallas_call x0 -> x1, Pallas kernels: none -> 117 us  [per_device(): pl.pallas_call(functools.partial(kernel, N, RN, H, G), out_shape=(jax.Sha...]
    reduce_scatter x2 -> x0, waiting for transfers between devices: 97.4 us -> none  [the longest x1 97.4 us: per_device(): lax.psum_scatter(jnp.dot(long_attn, w_rows, preferred_element_type=jnp.fl...]
    dot_general x18 -> x2, matrix products: 103 us -> 9.2 us  [the longest x1 7.15 us: per_device(): jnp.dot(l_attn, w_out, preferred_element_type=jnp.float32).astype(bf16)]
    all_gather x2 -> x0, waiting for transfers between devices: 59.8 us -> none  [the longest x1 56.5 us: prompt_attention(): value_piece = lax.all_gather(long_v, 'blk', axis=0, tiled=True)]
    all_to_all x1 -> x0, waiting for transfers between devices: 30 us -> none  [pack_attention(): lax.all_to_all(outgoing, 'blk', split_axis=0, concat_axis=0, tiled=True)]
    reduce_sum x9 -> x3, other arithmetic: 29.7 us -> 0.49 us  [the longest x1 0.21 us: per_device(): send_places = jnp.sum(jnp.where(picked, places[:, :, None], 0), axis=1)]
    dynamic_slice x7 -> x0, local copies, waits for them, and re-layouts: 18.8 us -> none  [one_step(): lax.dynamic_slice_in_dim(value_piece, block_start, step_rows, 0)]
    sub x2 -> x0, other arithmetic: 9.6 us -> none  [the longest x1 9.6 us: pack_attention(): weights = jnp.where(allowed, jnp.exp(scores - row_max[..., None]), 0.0)]
  transfers between devices with their start and end apart: 5 -> 0, of which waited for: 4 -> 0; matrix products, arithmetic and copies ran while one was open for 47% -> 0% of each run, Pallas kernels for 0% -> 0%
where the time goes in v1:
time: 135 us
  Pallas kernels  117 us (87%)
  matrix products  9.2 us (7%)
  local copies, waits for them, and re-layouts  6.2 us (5%)
  other arithmetic  1.46 us (1%)
    pallas_call x1, Pallas kernels, per_device(): pl.pallas_call(functools.partial(kernel, N, RN, H, G), out_shape=(jax.Sha...  117 us
    dot_general x1, matrix products, per_device(): jnp.dot(l_attn, w_out, preferred_element_type=jnp.float32).astype(bf16)  7.15 us
    unnamed x11, local copies, waits for them, and re-layouts  3.05 us

profile of v1, /device:TPU:14, one launch (start us, length us, event | category | flops | bytes accessed | tf_op | source)
XLA Modules:
  0.0 135.0 jit_solution(10212818640935094039)
XLA Ops:
  0.6 0.0 copy-start
  0.6 0.9 copy.19
  1.6 0.1 copy.20
  1.7 0.2 reduce_window_sum.11
  1.9 0.2 select_reduce_fusion.1
  2.1 0.1 reshape.154
  2.2 0.2 convert_reduce_fusion
  2.4 0.1 select_reduce_fusion
  2.5 0.1 broadcast_in_dim.46
  2.6 0.1 reshape.156
  2.7 0.7 pad_add_fusion
  3.4 0.8 copy.24.q_seg
  4.2 0.0 copy-done
  4.2 2.0 %gather_fusion = bf16[64,2,16,512]{3,2,1,0:T(8,128)(2,1)} fusion(bf16[64,2,16,512]{3,2,1,0:T(8,128)(2,1)S(1)} %copy-done, s32[1024]{0:T(1024)S(1)} %pad_clamp_fusion), kind=kCustom, calls=%fused_computation | custom fusion | bytes 4194560 | tf_op jit(solution)/shard_map/gather | solution.py:269
  6.3 0.0 copy-start.1
  6.3 1.0 copy-done.1
  7.3 0.0 copy-start.2
  7.3 1.0 copy-done.2
  8.4 0.0 slice-start
  8.4 117.4 %shard_map.113 = (bf16[256,2048]{1,0:T(8,128)(2,1)}, bf16[128,2048]{1,0:T(8,128)(2,1)S(1)}) custom-call(bf16[1024,512]{1,0:T(8,128)(2,1)} %long_q.1, bf16[1024,512]{1,0:T(8,128)(2,1)} %long_k.1, bf16[1024,512]{1,0:T(8,128)(2,1)} %long_v.1, bf16[8,8,2,16,512]{4,3,2,1,0:T(8,128)(2,1)} %bitcast.16, bf16[512,512]{1,0:T(8,128)(2,1)S(1)} %copy-done.1, ...), custom_call_target="tpu_custom_call" | custom-call | tf_op jit(solution)/shard_map/pallas_call | solution.py:283
  125.8 0.0 slice-start.1
  125.8 7.1 %convolution_convert_fusion = bf16[256,2048]{1,0:T(8,128)(2,1)} fusion(bf16[256,2048]{1,0:T(8,128)(2,1)} %get-tuple-element.4, bf16[2048,2048]{1,0:T(8,128)(2,1)} %param.19), kind=kOutput, calls=%fused_computation.1 | convolution fusion | flops 2148007936 | bytes 10485760 | tf_op jit(solution)/shard_map/dot_general | solution.py:299
  132.9 0.0 slice-done
  132.9 0.0 slice-done.1
  132.9 2.1 %convolution_convert_fusion.1 = bf16[128,2048]{1,0:T(8,128)(2,1)} fusion(bf16[128,2048]{1,0:T(8,128)(2,1)S(1)} %get-tuple-element.5, bf16[2048,2048]{1,0:T(8,128)(2,1)S(1)} %bitcast.15), kind=kOutput, calls=%fused_computation.2 | convolution fusion | flops 1074003968 | bytes 9437184 | tf_op jit(solution)/shard_map/dot_general | solution.py:300
  (8 shorter events, 0.1 us)
Async XLA Ops:
  0.6 3.6 %copy-start = (bf16[64,2,16,512]{3,2,1,0:T(8,128)(2,1)S(1)}, bf16[64,2,16,512]{3,2,1,0:T(8,128)(2,1)}, u32[]{:S(2)}) copy-start(bf16[64,2,16,512]{3,2,1,0:T(8,128)(2,1)} %param.17) | copy-start | bytes 6291460
  6.3 1.0 copy-start.1
  7.3 1.0 copy-start.2
  8.4 124.6 %slice-start = ((s8[8388608]{0:T(1024)(128)(4,1)}), s8[4194304]{0:T(1024)(128)(4,1)S(1)}, s32[]{:S(2)}) async-start(s8[8388608]{0:T(1024)(128)(4,1)} %bitcast.14), calls=%async_computation | async-start | bytes 8388608
  125.8 7.2 %slice-start.1 = ((s8[8388608]{0:T(1024)(128)(4,1)}), s8[4194304]{0:T(1024)(128)(4,1)S(1)}, s32[]{:S(2)}) async-start(s8[8388608]{0:T(1024)(128)(4,1)} %bitcast.14), calls=%async_computation.1 | async-start | bytes 8388608

commit v2 on v1

--- a/solution.py
+++ b/solution.py
@@ -25,9 +25,9 @@
     return lax.dot_general(q, k, (((1,), (1,)), ((), ())), preferred_element_type=jnp.float32)
 
 
-def kernel(N, RN, H, G, long_q, long_k, long_v, pages_out, sq, sk, sv, q_seg, k_seg,
-           l_out, s_out, kbuf, vbuf, qbuf, obuf, pbuf, sbuf,
-           kv_send, kv_recv, fwd_send, q_send, q_recv, p_send, p_recv,
+def kernel(N, RN, H, G, long_q, long_k, long_v, pages_out, short_q, short_k, short_v, w_hbm, q_seg, k_seg,
+           long_res, short_res, kbuf, vbuf, qbuf, obuf, pbuf, sbuf, sq, sk, sv, w_out, l_out, s_out,
+           m_keep, l_keep, a_keep, local_sem, kv_send, kv_recv, fwd_send, q_send, q_recv, p_send, p_recv,
            o_send, o_recv, s_send, s_recv):
     d = lax.axis_index("blk")
     req = lax.axis_index("req")
@@ -39,6 +39,13 @@
     total = N * RN
     me = d * RN + req
 
+    def local_copies():
+        return [pltpu.make_async_copy(src, dst, local_sem.at[i]) for i, (src, dst) in enumerate(
+            ((short_q, sq), (short_k, sk), (short_v, sv), (w_hbm, w_out)))]
+
+    for copy in local_copies():
+        copy.start()
+
     barrier = pltpu.get_barrier_semaphore()
 
     @pl.loop(1, total)
@@ -90,9 +97,6 @@
         return pltpu.make_async_remote_copy(
             pages_out.at[other], pbuf.at[d], p_send.at[k], p_recv.at[d],
             device_id=(other, req), device_id_type=MESH)
-
-    for k in range(N):
-        page_copy(k).start()
 
     def arrived(buf, b, sem):
         pltpu.make_async_copy(buf.at[b], buf.at[b], sem).wait()
@@ -133,6 +137,29 @@
 
     def block_of(j):
         return j * G + (j % 2) * (G - 1 - 2 * p) + p
+
+    cache_len = k_seg.shape[1] - sk.shape[0]
+    pack = sbuf.shape[0]
+    ts = min(256, pack)
+
+    for copy in local_copies()[:3]:
+        copy.wait()
+
+    @pl.loop(0, H)
+    def _(h):
+        cols = head_cols(h)
+        for t in range(pack // ts):
+            rows = pl.ds(t * ts, ts)
+            keys = (t + 1) * ts
+            own = jnp.logical_and(
+                k_seg[:, pl.ds(cache_len, keys)] == q_seg[rows, :],
+                lax.broadcasted_iota(jnp.int32, (ts, keys), 1)
+                <= lax.broadcasted_iota(jnp.int32, (ts, keys), 0) + t * ts)
+            m, l, acc = step(
+                empty(ts), sq[rows, cols], sk[pl.ds(0, keys), cols], sv[pl.ds(0, keys), cols], own)
+            m_keep[h, rows, :] = jnp.broadcast_to(m, (ts, HD))
+            l_keep[h, rows, :] = l
+            a_keep[h, rows, :] = acc
 
     @pl.loop(0, H)
     def _(j):
@@ -147,16 +174,29 @@
             for which, buf in ((0, kbuf), (1, vbuf)):
                 arrived(buf, theirs, kv_recv.at[which, theirs])
         arrived(qbuf, j, q_recv.at[j])
+
+        @pl.when(j == 0)
+        def _():
+            for k in range(N):
+                page_copy(k).start()
+
+        states = []
         for t in range(R // tq):
-            rows = pl.ds(t * tq, tq)
-            q = qbuf[j, rows, :]
             keys = (t + 1) * tq
             mask = (lax.broadcasted_iota(jnp.int32, (tq, keys), 1)
                     <= lax.broadcasted_iota(jnp.int32, (tq, keys), 0) + t * tq)
-            state = step(empty(tq), q, kbuf[b, pl.ds(0, keys), :], vbuf[b, pl.ds(0, keys), :], mask)
-            state = lax.fori_loop(
-                0, b, lambda i, st: step(st, q, kbuf[i], vbuf[i], None), state)
-            obuf[j, rows, :] = finish(state)
+            states.append(step(
+                empty(tq), qbuf[j, pl.ds(t * tq, tq), :],
+                kbuf[b, pl.ds(0, keys), :], vbuf[b, pl.ds(0, keys), :], mask))
+
+        def one_block(i, now):
+            k, v = kbuf[i], vbuf[i]
+            return tuple(
+                step(now[t], qbuf[j, pl.ds(t * tq, tq), :], k, v, None) for t in range(R // tq))
+
+        states = lax.fori_loop(0, b, one_block, tuple(states))
+        for t in range(R // tq):
+            obuf[j, pl.ds(t * tq, tq), :] = finish(states[t])
         for r in range(RN):
             here = jnp.logical_and(b == d, req == r)
 
@@ -172,10 +212,6 @@
 
     for k in range(N):
         arrived(pbuf, (d + k) % N, p_recv.at[(d + k) % N])
-
-    cache_len = k_seg.shape[1] - sk.shape[0]
-    pack = sbuf.shape[0]
-    ts = min(256, pack)
 
     @pl.loop(0, H)
     def _(h):
@@ -184,15 +220,9 @@
         cv = pbuf[:, :, 1, :, cols].reshape(cache_len, HD)
         for t in range(pack // ts):
             rows = pl.ds(t * ts, ts)
-            keys = (t + 1) * ts
-            q = sq[rows, cols]
-            seg = q_seg[rows, :]
-            own = jnp.logical_and(
-                k_seg[:, pl.ds(cache_len, keys)] == seg,
-                lax.broadcasted_iota(jnp.int32, (ts, keys), 1)
-                <= lax.broadcasted_iota(jnp.int32, (ts, keys), 0) + t * ts)
-            state = step(empty(ts), q, sk[pl.ds(0, keys), cols], sv[pl.ds(0, keys), cols], own)
-            state = step(state, q, ck, cv, k_seg[:, pl.ds(0, cache_len)] == seg)
+            state = (m_keep[h, rows, :][:, :1], l_keep[h, rows, :], a_keep[h, rows, :])
+            state = step(
+                state, sq[rows, cols], ck, cv, k_seg[:, pl.ds(0, cache_len)] == q_seg[rows, :])
             sbuf[rows, cols] = finish(state)
 
     def short_copy(k):
@@ -207,16 +237,32 @@
 
     for k in range(RN):
         short_copy(k).start()
+    local_copies()[3].wait()
+    WHOLE = l_out.shape[1]
+    nt = min(512, WHOLE)
+
+    def project(attn, result):
+        @pl.loop(0, WHOLE // nt)
+        def _(n):
+            cols = pl.ds(pl.multiple_of(n * nt, nt), nt)
+            result[:, cols] = jnp.dot(
+                attn[...], w_out[:, cols], preferred_element_type=jnp.float32
+            ).astype(jnp.bfloat16)
+
+    @pl.loop(0, RN * H)
+    def _(i):
+        dst = l_out.at[:, head_cols(i)]
+        pltpu.make_async_copy(dst, dst, o_recv.at[i]).wait()
+
+    project(l_out, long_res)
+
     for k in range(RN):
         r = (req + k) % RN
         W = sbuf.shape[1]
         dst = s_out.at[:, pl.ds(pl.multiple_of(r * W, W), W)]
         pltpu.make_async_copy(dst, dst, s_recv.at[r]).wait()
 
-    @pl.loop(0, RN * H)
-    def _(i):
-        dst = l_out.at[:, head_cols(i)]
-        pltpu.make_async_copy(dst, dst, o_recv.at[i]).wait()
+    project(s_out, short_res)
 
     for k in range(1, RN):
         short_copy(k).wait_send()
@@ -280,24 +326,27 @@
     vmem = pl.BlockSpec(memory_space=pltpu.VMEM)
     anywhere = pl.BlockSpec(memory_space=pl.ANY)
     bf16 = jnp.bfloat16
-    l_attn, s_attn = pl.pallas_call(
+    return pl.pallas_call(
         functools.partial(kernel, N, RN, H, G),
         out_shape=(jax.ShapeDtypeStruct((R // RN, W * RN), bf16),
                    jax.ShapeDtypeStruct((pack // RN, W * RN), bf16)),
-        in_specs=[anywhere] * 4 + [vmem] * 5,
-        out_specs=(anywhere, anywhere),
+        in_specs=[anywhere] * 8 + [vmem] * 2,
+        out_specs=(vmem, vmem),
         scratch_shapes=[
             pltpu.VMEM((N, R, HD), bf16), pltpu.VMEM((N, R, HD), bf16),
             pltpu.VMEM((H, R, HD), bf16), pltpu.VMEM((H, R, HD), bf16),
             pltpu.VMEM((N, cap, 2, page_len, W), bf16), pltpu.VMEM((pack, W), bf16),
+            pltpu.VMEM((pack, W), bf16), pltpu.VMEM((pack, W), bf16), pltpu.VMEM((pack, W), bf16),
+            pltpu.VMEM(w_out.shape, bf16),
+            pltpu.VMEM((R // RN, W * RN), bf16), pltpu.VMEM((pack // RN, W * RN), bf16),
+            pltpu.VMEM((H, pack, HD), jnp.float32), pltpu.VMEM((H, pack, HD), jnp.float32),
+            pltpu.VMEM((H, pack, HD), jnp.float32), DMA((4,)),
             DMA((2, H)), DMA((2, N)), DMA((2, H, G)), DMA((H,)), DMA((H,)),
             DMA((N,)), DMA((N,)), DMA((H, RN)), DMA((RN * H,)), DMA((RN,)), DMA((RN,)),
         ],
         compiler_params=pltpu.CompilerParams(
             collective_id=0, has_side_effects=True, vmem_limit_bytes=52 * 2**20),
-    )(long_q, long_k, long_v, outgoing, short_q, short_k, short_v, q_seg, k_seg)
-    return (jnp.dot(l_attn, w_out, preferred_element_type=jnp.float32).astype(bf16),
-            jnp.dot(s_attn, w_out, preferred_element_type=jnp.float32).astype(bf16))
+    )(long_q, long_k, long_v, outgoing, short_q, short_k, short_v, w_out, q_seg, k_seg)
 
 
 def solution(mesh):

time: 135 us -> 121 us (0.90)
  matrix products: 9.2 us -> 0 us
  Pallas kernels: 117 us -> 111 us
    dot_general x2 -> x0, matrix products: 9.2 us -> none  [the longest x1 7.15 us: per_device(): jnp.dot(l_attn, w_out, preferred_element_type=jnp.float32).astype(bf16)]
    pallas_call x1, Pallas kernels: 117 us -> 111 us  [per_device(): pl.pallas_call(functools.partial(kernel, N, RN, H, G), out_shape=(jax.Sha...]
    unnamed x11 -> x9, local copies, waits for them, and re-layouts: 3.05 us -> 4.06 us
where the time goes in v2:
time: 121 us
  Pallas kernels  111 us (92%)
  local copies, waits for them, and re-layouts  7.22 us (6%)
  other arithmetic  1.46 us (1%)
    pallas_call x1, Pallas kernels, per_device(): pl.pallas_call(functools.partial(kernel, N, RN, H, G), out_shape=(jax.Sha...  111 us
    unnamed x9, local copies, waits for them, and re-layouts  4.06 us

profile of v2, /device:TPU:14, one launch (start us, length us, event | category | flops | bytes accessed | tf_op | source)
XLA Modules:
  0.0 120.6 jit_solution(11735134581925454655)
XLA Ops:
  0.6 0.0 copy-start
  0.6 0.9 copy.19
  1.6 0.1 copy.20
  1.7 0.2 reduce_window_sum.11
  1.9 0.2 select_reduce_fusion.1
  2.1 0.1 reshape.154
  2.2 0.2 convert_reduce_fusion
  2.4 0.1 select_reduce_fusion
  2.5 0.1 broadcast_in_dim.46
  2.6 0.1 reshape.156
  2.7 0.7 pad_add_fusion
  3.4 0.8 copy.24.q_seg
  4.2 0.0 copy-done
  4.2 0.0 copy-start.1
  4.2 0.0 copy-start.2
  4.3 2.0 %gather_fusion = bf16[64,2,16,512]{3,2,1,0:T(8,128)(2,1)} fusion(bf16[64,2,16,512]{3,2,1,0:T(8,128)(2,1)S(1)} %copy-done, s32[1024]{0:T(1024)S(1)} %pad_clamp_fusion), kind=kCustom, calls=%fused_computation | custom fusion | bytes 4194560 | tf_op jit(solution)/shard_map/gather | solution.py:315
  6.3 0.0 copy-done.1
  6.3 0.0 copy-done.2
  6.3 111.2 %shard_map.113 = (bf16[256,2048]{1,0:T(8,128)(2,1)}, bf16[128,2048]{1,0:T(8,128)(2,1)S(1)}) custom-call(bf16[1024,512]{1,0:T(8,128)(2,1)} %long_q.1, bf16[1024,512]{1,0:T(8,128)(2,1)} %long_k.1, bf16[1024,512]{1,0:T(8,128)(2,1)} %long_v.1, bf16[8,8,2,16,512]{4,3,2,1,0:T(8,128)(2,1)} %bitcast.10, bf16[512,512]{1,0:T(8,128)(2,1)S(1)} %copy-done.1, ...), custom_call_target="tpu_custom_call" | custom-call | tf_op jit(solution)/shard_map/pallas_call | solution.py:329
  117.5 2.3 %copy.27 = bf16[256,2048]{1,0:T(8,128)(2,1)} copy(bf16[256,2048]{1,0:T(8,128)(2,1)} %get-tuple-element.11) | data formatting | bytes 2097152
  119.8 0.8 copy.28
  (7 shorter events, 0.1 us)
Async XLA Ops:
  0.6 3.6 %copy-start = (bf16[64,2,16,512]{3,2,1,0:T(8,128)(2,1)S(1)}, bf16[64,2,16,512]{3,2,1,0:T(8,128)(2,1)}, u32[]{:S(2)}) copy-start(bf16[64,2,16,512]{3,2,1,0:T(8,128)(2,1)} %param.17) | copy-start | bytes 6291460
  4.2 2.1 %copy-start.1 = (bf16[512,512]{1,0:T(8,128)(2,1)S(1)}, bf16[512,512]{1,0:T(8,128)(2,1)}, u32[]{:S(2)}) copy-start(bf16[512,512]{1,0:T(8,128)(2,1)} %short_q.1) | copy-start | bytes 1572868
  4.2 2.0 %copy-start.2 = (bf16[512,512]{1,0:T(8,128)(2,1)S(1)}, bf16[512,512]{1,0:T(8,128)(2,1)}, u32[]{:S(2)}) copy-start(bf16[512,512]{1,0:T(8,128)(2,1)} %short_k.1) | copy-start | bytes 1572868
